TPU v7x, 32 devices: a whole 2x2x4 slice. The times are simulated.
32 devices in a mesh: groups: 2 (over x), rep: 2 (over core), tp: 8 (over z, y).
Axes of the slice: x: 2, y: 2, z: 4, core: 2. Of those that a mesh axis runs over, the one named last changes fastest.
Arguments:
- hidden: bfloat16 [1024, 2, 28672], P(('groups', 'rep'), None, 'tp'), parts along dimension 0, may hold values from -6 to 6
- down_weight: bfloat16 [28672, 8192], P('tp'), may hold values from -0.046875 to 0.046875
- residual: bfloat16 [1024, 2, 8192], P(('groups', 'rep'), None, 'tp'), parts along dimension 0, may hold values from -6 to 6
- pool_shrink: bfloat16 [16, 8, 64, 3584], P(('rep', 'tp')), may hold values from -0.03125 to 0.03125
- pool_expand: bfloat16 [16, 8, 64, 1024], P(('rep', 'tp')), may hold values from -0.75 to 0.75
- tenant_home: int32 [16], replicated, may hold values from 0 to 15, each once
- request_owner_tenant: int32 [1024, 1], P(('groups', 'rep')), parts along dimension 0, may hold values from 0 to 15; in each aligned block of 256 rows (0 to 255, 256 to 511, ...) at most 64 rows name the same one
Outputs:
- mixed: bfloat16 [1024, 2, 8192], P(('groups', 'rep'), None, 'tp'), parts along dimension 0
There are 2 independent parts, one for each index of `groups`. A program takes and returns all parts, laid end to end along the dimension named above; an argument that names none is the same for every part. Nothing has to cross between parts.
Inputs may be any that keep to these rules, and one draw needn't show every extreme that they name: `request_owner_tenant`: among the 256 requests of one replica no tenant appears more than 64 times, and in some replica one tenant appears exactly 64 times; every tenant appears in some request. `tenant_home`: each tenant has its own home.
All inputs are finite; a program needn't handle non-finite values.
Results may differ from a plain program's by a relative error of at most 0.0033.
Values may be sent and summed in bfloat16 or wider, within the bound.
A program may use at most 448 MiB of HBM per device.

v0:
```python
import jax
import jax.numpy as jnp
from jax import lax
from jax.sharding import PartitionSpec as P


def per_device(
    hidden, down_weight, residual, pool_shrink, pool_expand, tenant_home, request_owner_tenant
):
    tp_count = lax.axis_size("tp")
    replica_count = lax.axis_size("rep")
    dev_count = tp_count * replica_count
    tp_place = lax.axis_index("tp")
    requests, step_count, unit_width = hidden.shape
    feature_width = residual.shape[2]
    code_width = pool_shrink.shape[2]
    tenant_ids = request_owner_tenant[:, 0]
    home_device = (
        tenant_home // tp_count * tp_count + (tenant_home % tp_count + tp_place) % tp_count
    )
    source_device_of = home_device[tenant_ids]
    flat_hidden = hidden.reshape(requests * step_count, unit_width)
    base_share = lax.psum_scatter(
        lax.dot_general(
            down_weight, flat_hidden, (((0,), (1,)), ((), ())), preferred_element_type=jnp.float32
        ),
        "tp",
        scatter_dimension=0,
        tiled=True,
    )
    base_share = jnp.transpose(base_share).reshape(requests, step_count, feature_width)
    shrink_out = jnp.broadcast_to(pool_shrink, (replica_count,) + pool_shrink.shape[1:])
    expand_out = jnp.broadcast_to(pool_expand, (replica_count,) + pool_expand.shape[1:])
    shrink_flat = shrink_out.reshape(dev_count, code_width, unit_width)
    expand_flat = expand_out.reshape(dev_count, code_width, feature_width)
    received_shrink, received_expand = (
        lax.all_to_all(shrink_flat, ("rep", "tp"), split_axis=0, concat_axis=0, tiled=True),
        lax.all_to_all(expand_flat, ("rep", "tp"), split_axis=0, concat_axis=0, tiled=True),
    )
    row_shrink = received_shrink[source_device_of]
    code_part = jnp.einsum("isf,ikf->isk", hidden, row_shrink, preferred_element_type=jnp.float32)
    codes = lax.psum(code_part, "tp").astype(jnp.bfloat16)
    row_expand = received_expand[source_device_of]
    adapted = jnp.einsum("isk,ikc->isc", codes, row_expand, preferred_element_type=jnp.float32)
    return (residual.astype(jnp.float32) + base_share + adapted).astype(jnp.bfloat16)


def solution(mesh):
    in_specs = (
        P(("groups", "rep"), None, "tp"),
        P("tp", None),
        P(("groups", "rep"), None, "tp"),
        P(("rep", "tp"), None, None, None),
        P(("rep", "tp"), None, None, None),
        P(),
        P(("groups", "rep"), None),
    )
    out_specs = P(("groups", "rep"), None, "tp")
    return jax.shard_map(
        per_device, mesh=mesh, in_specs=in_specs, out_specs=out_specs, check_vma=False
    )
```

profile of v0, /device:TPU:0, one launch (start us, length us, event | category | flops | bytes accessed | tf_op | source)
XLA Modules:
  0.0 562.0 jit_solution(11029033713449002044)
XLA Ops:
  6.5 0.0 reduce-scatter.2.cloned.1.call-start
  6.5 8.4 %reshape.25 = bf16[512,3584]{1,0:T(8,128)(2,1)} reshape(bf16[256,2,3584]{2,1,0:T(2,128)(2,1)} %param.7) | data formatting | bytes 7340032 | tf_op jit(solution)/shard_map/reshape | solution.py:22
  14.9 39.7 %fusion.5 = f32[8192,512]{1,0:T(8,128)} fusion(bf16[3584,8192]{1,0:T(8,128)(2,1)} %param.8, bf16[512,3584]{1,0:T(8,128)(2,1)} %reshape.25), kind=kOutput, calls=%fused_computation.36 | convolution fusion | flops 30064771072 | bytes 79167488 | tf_op jit(solution)/shard_map/dot_general | solution.py:24
  54.6 0.0 copy-start.1
  54.6 0.0 reduce-scatter.2.cloned.1.call-update
  54.6 0.0 copy-start
  54.6 1.2 copy-done.1
  55.8 0.3 broadcast_in_dim.20
  56.1 103.7 %all_to_all.10 = bf16[16,64,1024]{2,1,0:T(8,128)(2,1)S(1)} all-to-all(bf16[16,64,1024]{2,1,0:T(8,128)(2,1)S(1)} %bitcast.33), channel_id=1, replica_groups=mesh['groups'=2,'rep'=2,'tp'=8] {'rep','tp'}, dimensions={0} | all-to-all | bytes 4194304 | tf_op jit(solution)/shard_map/all_to_all | solution.py:38
  159.8 0.0 copy-done
  159.8 3.7 broadcast_in_dim.18
  163.5 0.0 copy-start.4
  163.5 0.0 copy-start.2
  163.5 5.0 all-to-all-start
  168.6 0.0 copy-done.4
  168.6 0.7 fusion.4
  169.3 0.0 copy-done.2
  169.3 4.3 compare_select_fusion.2
  173.7 5.8 %select_select_fusion = s32[256]{0:T(256)S(1)} fusion(pred[256]{0:T(512)(128)(4,1)S(1)} %get-tuple-element.13, pred[256]{0:T(512)(128)(4,1)S(1)} %get-tuple-element.12, pred[256]{0:T(512)(128)(4,1)S(1)} %get-tuple-element.11, pred[256]{0:T(512)(128)(4,1)S(1)} %get-tuple-element.10, pred[256]{0:T(512)(128)(4,1)S(1)} %get-tuple-element.9, ...), kind=kLoop, calls=%fused_computation.31 | loop fusion | flops 2304 | bytes 4388 | tf_op jit(solution)/shard_map/gather | solution.py:21
  179.5 13.8 %gather_fusion.1 = bf16[256,64,1024]{2,1,0:T(8,128)(2,1)} fusion(bf16[16,64,1024]{2,1,0:T(8,128)(2,1)S(1)} %all_to_all.10, s32[1024]{0:T(1024)S(1)} %pad_clamp_fusion), kind=kCustom, calls=%fused_computation.1 | custom fusion | bytes 67109888 | tf_op jit(solution)/shard_map/gather | solution.py:43
  193.3 202.3 %all-to-all-done = bf16[16,64,3584]{2,1,0:T(8,128)(2,1)} async-done(((bf16[16,64,3584]{2,1,0:T(8,128)(2,1)}), bf16[16,64,3584]{2,1,0:T(8,128)(2,1)}, u32[]{:S(2)}, u32[]{:S(2)}) %all-to-all-start) | async-done | bytes 7340064 | tf_op jit(solution)/shard_map/all_to_all | solution.py:37
  395.7 42.1 %gather_fusion = bf16[256,64,3584]{2,1,0:T(8,128)(2,1)} fusion(bf16[16,64,3584]{2,1,0:T(8,128)(2,1)} %all-to-all-done, s32[1024]{0:T(1024)S(1)} %pad_clamp_fusion), kind=kCustom, calls=%fused_computation | custom fusion | bytes 234882048 | tf_op jit(solution)/shard_map/gather | solution.py:40
  437.8 51.1 %convolution_bitcast_fusion = f32[256,2,64]{2,1,0:T(2,128)S(1)} fusion(bf16[256,64,3584]{2,1,0:T(8,128)(2,1)} %gather_fusion, bf16[256,2,3584]{2,1,0:T(2,128)(2,1)} %param.7), kind=kOutput, calls=%fused_computation.3 | convolution fusion | flops 234881024 | bytes 121241600 | tf_op jit(solution)/shard_map/isf,ikf->isk/dot_general | solution.py:41
  488.9 0.0 copy-start.3
  488.9 47.6 %all-reduce.1 = bf16[256,2,64]{2,1,0:T(2,128)(2,1)S(1)} all-reduce(f32[256,2,64]{2,1,0:T(2,128)S(1)} %convolution_bitcast_fusion), channel_id=1, replica_groups=mesh['groups'=2,'rep'=2,'tp'=8] {'tp'}, use_global_device_ids=true, to_apply=%region_1.2 | all-reduce | flops 32768 | bytes 196608 | tf_op jit(solution)/shard_map/psum | solution.py:42
  536.5 0.0 reduce-scatter.2.cloned.1.call-done
  536.6 1.9 copy.9
  538.5 2.3 reshape.26
  540.8 0.0 copy-done.3
  540.8 14.3 %add_convert_fusion = bf16[256,2,1024]{2,1,0:T(2,128)(2,1)} fusion(f32[256,2,1024]{2,1,0:T(2,128)} %reshape.26, bf16[256,2,1024]{2,1,0:T(2,128)(2,1)S(1)} %copy-done.3, bf16[256,64,1024]{2,1,0:T(8,128)(2,1)} %gather_fusion.1, bf16[256,2,64]{2,1,0:T(2,128)(2,1)S(1)} %all-reduce.1), kind=kOutput, calls=%fused_computation.2 | convolution fusion | flops 69206016 | bytes 37814272 | tf_op jit(solution)/shard_map/isk,ikc->isc/dot_general | solution.py:44
  (4 shorter events, 0.1 us)
Async XLA Ops:
  6.5 530.0 %reduce-scatter.2.cloned.1.call-start = ((), (), s32[]{:S(2)}) async-start(), calls=%async_computation.3 | async-start | bytes 18874368 | tf_op jit(solution)/shard_map/reduce_scatter | solution.py:23
  54.6 1.2 copy-start.1
  54.6 105.2 %copy-start = (bf16[1,8,64,3584]{3,2,1,0:T(8,128)(2,1)S(1)}, bf16[1,8,64,3584]{3,2,1,0:T(8,128)(2,1)}, u32[]{:S(2)}) copy-start(bf16[1,8,64,3584]{3,2,1,0:T(8,128)(2,1)} %param.10) | copy-start | bytes 11010052
  163.5 5.0 copy-start.4
  163.5 5.8 %copy-start.2 = (s32[256,1]{0,1:T(1,128)S(1)}, s32[256,1]{0,1:T(1,128)}, u32[]{:S(2)}) copy-start(s32[256,1]{0,1:T(1,128)} %param.13) | copy-start | bytes 3076
  163.5 232.2 %all-to-all-start = ((bf16[16,64,3584]{2,1,0:T(8,128)(2,1)}), bf16[16,64,3584]{2,1,0:T(8,128)(2,1)}, u32[]{:S(2)}, u32[]{:S(2)}) async-start(bf16[16,64,3584]{2,1,0:T(8,128)(2,1)} %bitcast.32), calls=%async_computation.1 | async-start | bytes 14680064 | tf_op jit(solution)/shard_map/all_to_all | solution.py:37
  488.9 51.9 %copy-start.3 = (bf16[256,2,1024]{2,1,0:T(2,128)(2,1)S(1)}, bf16[256,2,1024]{2,1,0:T(2,128)(2,1)}, u32[]{:S(2)}) copy-start(bf16[256,2,1024]{2,1,0:T(2,128)(2,1)} %param.9) | copy-start | bytes 3145732
Sparse Core Ops, SparseCore 0:
  54.7 467.3 reduce-scatter.1
where the time goes:
time: 563 us; the launch traced here: 562 us
  waiting for transfers between devices  202 us (36%)
  blocking collectives  151 us (27%)
  matrix products  105 us (19%)
  local copies, waits for them, and re-layouts  74.4 us (13%)
  between operations  13.5 us (2%)
  other arithmetic  10.2 us (2%)
    all_to_all x1, waiting for transfers between devices, per_device(): lax.all_to_all(shrink_flat, ('rep', 'tp'), split_axis=0, concat_axis=0, t...  202 us
    all_to_all x1, blocking collectives, per_device(): lax.all_to_all(expand_flat, ('rep', 'tp'), split_axis=0, concat_axis=0, t...  104 us
    dot_general x1, matrix products, per_device(): jnp.einsum('isf,ikf->isk', hidden, row_shrink, preferred_element_type=jnp...  51.1 us
    psum x1, blocking collectives, per_device(): codes = lax.psum(code_part, 'tp').astype(jnp.bfloat16)  47.6 us
    gather x1, local copies, waits for them, and re-layouts, per_device(): row_shrink = received_shrink[source_device_of]  42.1 us
    dot_general x1, matrix products, per_device(): lax.dot_general(down_weight, flat_hidden, (((0,), (1,)), ((), ())), prefe...  39.7 us
    dot_general x1, matrix products, per_device(): jnp.einsum('isk,ikc->isc', codes, row_expand, preferred_element_type=jnp....  14.3 us
    gather x1, local copies, waits for them, and re-layouts, per_device(): row_expand = received_expand[source_device_of]  13.8 us
  transfers between devices with their start and end apart: 2, of which 1 were waited for; matrix products, arithmetic and copies ran while one was open for 22% of the time, Pallas kernels for 0%

commit v1 on v0

v1 whole, which is shorter than its diff:
```python
import functools
import math

import jax
import jax.numpy as jnp
from jax import lax
from jax.experimental import pallas as pl
from jax.experimental.pallas import tpu as pltpu
from jax.sharding import PartitionSpec as P

MESH = pl.DeviceIdType.MESH
F32 = jnp.float32
BF16 = jnp.bfloat16


def fused(
    tp, lo, hi, tile, sub,
    hidden, weight, shrink, expand, source, out,
    w_buf, y_send, y_recv, keep, z_send, z_recv, a_buf, e_buf, part, part_in, code, code_own,
    w_sem, y_ssem, y_rsem, z_ssem, z_rsem, a_sems, e_sems, c_sems,
):
    g, r, p = lax.axis_index("groups"), lax.axis_index("rep"), lax.axis_index("tp")
    z, y = p // lo, p % lo
    rows = hidden.shape[0]
    width = out.shape[1]
    per = width // tile
    units = hi * per
    rank = shrink.shape[2]
    half = rank // 2
    share = rows // tp
    across, sibling = {"groups": 1 - g}, {"rep": 1 - r}

    def remote(src, dst, ssem, rsem, device):
        return pltpu.make_async_remote_copy(
            src_ref=src, dst_ref=dst, send_sem=ssem, recv_sem=rsem,
            device_id=device, device_id_type=MESH,
        )

    def loop(n, body):
        lax.fori_loop(0, n, lambda i, c: (body(i), c)[1], 0)

    def peer(j):
        return {"tp": (p + j) % tp}

    barrier = pltpu.get_barrier_semaphore()
    loop(tp - 1, lambda j: pl.semaphore_signal(
        barrier, inc=1, device_id=peer(j + 1), device_id_type=MESH))
    pl.semaphore_signal(barrier, inc=1, device_id=across, device_id_type=MESH)
    pl.semaphore_signal(barrier, inc=1, device_id=sibling, device_id_type=MESH)

    def unit(i):
        q, c = i // per, i % per
        zz = jnp.where(q % 2 == 0, hi - 1 - q // 2, q // 2)
        return zz, c

    sends = units * (lo - 1)
    total = units * lo

    def tile_of(n):
        sending = n < sends
        i = jnp.where(sending, n // max(lo - 1, 1), n - sends)
        j = jnp.where(sending, 1 + n % max(lo - 1, 1), 0)
        zz, c = unit(i)
        return zz, c, j

    def w_copy(n):
        zz, c, j = tile_of(n)
        column = (zz * lo + (y + j) % lo) * width + c * tile
        return pltpu.make_async_copy(
            weight.at[:, pl.ds(pl.multiple_of(column, tile), tile)],
            w_buf.at[n % 2], w_sem.at[n % 2],
        )

    w_copy(0).start()
    pl.semaphore_wait(barrier, tp + 1)

    mine = pl.ds(pl.multiple_of(g * half, half), half)
    other = pl.ds(pl.multiple_of((1 - g) * half, half), half)

    def page_copies(j):
        k = (p + j) % tp
        return [
            remote(pool.at[0, k, mine], buf.at[r, p, mine], s.at[0, k], s.at[1, p], {"tp": k})
            for pool, buf, s in ((shrink, a_buf, a_sems), (expand, e_buf, e_sems))
        ]

    def own_copies():
        return [
            pltpu.make_async_copy(pool.at[0, p, mine], buf.at[r, p, mine], s.at[1, p])
            for pool, buf, s in ((shrink, a_buf, a_sems), (expand, e_buf, e_sems))
        ]

    def across_copies(src, rows_of):
        return [
            remote(buf.at[r, src, rows_of], buf.at[r, src, rows_of],
                   s.at[2, src], s.at[3, src], across)
            for buf, s in ((a_buf, a_sems), (e_buf, e_sems))
        ]

    def sibling_copies(rep, src):
        return [
            remote(buf.at[rep, src], buf.at[rep, src], s.at[4, src], s.at[5, src], sibling)
            for buf, s in ((a_buf, a_sems), (e_buf, e_sems))
        ]

    def start_pages(j):
        for copy in page_copies(j + 1):
            copy.start()

    for copy in own_copies():
        copy.start()
    loop(tp - 1, start_pages)

    def product(n, store):
        @pl.when(n + 1 < total)
        def _():
            w_copy(n + 1).start()

        w_copy(n).wait()

        def piece(t):
            columns = pl.ds(pl.multiple_of(t * sub, sub), sub)
            store(columns, jnp.dot(
                hidden[...], w_buf[n % 2, :, columns], preferred_element_type=F32))

        loop(tile // sub, piece)

    def y_copy(u, j):
        device = {"tp": z * lo + (y + j) % lo}
        return remote(y_send.at[u, j - 1], y_recv.at[u, j - 1],
                      y_ssem.at[u, j - 1], y_rsem.at[u, j - 1], device)

    def send_tile(n):
        zz, c, j = tile_of(n)
        u = zz * per + c

        def store(columns, value):
            y_send[u, j - 1, :, columns] = value.astype(BF16)

        product(n, store)
        y_copy(u, j).start()

    loop(sends, send_tile)

    def forward(j):
        src = (p + tp - j) % tp

        @pl.when(j == 0)
        def _():
            for copy in own_copies():
                copy.wait()

        @pl.when(j > 0)
        def _():
            for pool, buf, s in ((shrink, a_buf, a_sems), (expand, e_buf, e_sems)):
                remote(pool.at[0, src, mine], buf.at[r, src, mine],
                       s.at[0, src], s.at[1, src], {"tp": src}).wait_recv()

        for copy in across_copies(src, mine):
            copy.start()

    def keep_tile(i):
        zz, c = unit(i)
        u = zz * per + c

        def store(columns, value):
            keep[u, :, columns] = value

        product(sends + i, store)
        loop(tp // units, lambda t: forward(i * (tp // units) + t))

    loop(units, keep_tile)

    def base(u):
        value = keep[u]
        for j in range(1, lo):
            value = value + y_recv[u, j - 1].astype(F32)
        return value

    def wait_y(u):
        for j in range(1, lo):
            y_copy(u, j).wait_recv()

    def z_copy(u, zz, c):
        nz = jnp.where(zz > z, z + 1, z - 1)
        slot = jnp.where((nz == zz) & (zz < z), units + c, u)
        return remote(z_send.at[u], z_recv.at[slot], z_ssem.at[u], z_rsem.at[slot],
                      {"tp": nz * lo + y})

    def z_arrived(slot):
        remote(z_send.at[0], z_recv.at[slot], z_ssem.at[0], z_rsem.at[slot],
               across).wait_recv()

    def pass_on(i):
        zz, c = unit(i)
        u = zz * per + c
        first = jnp.where(zz > z, z == 0, z == hi - 1)

        @pl.when(zz != z)
        def _():
            wait_y(u)

            @pl.when(first)
            def _():
                z_send[u] = base(u).astype(BF16)

            @pl.when(jnp.logical_not(first))
            def _():
                z_arrived(u)
                z_send[u] = (base(u) + z_recv[u].astype(F32)).astype(BF16)

            z_copy(u, zz, c).start()

    def share_page(j):
        src = (p + tp - j) % tp
        for copy in across_copies(src, other):
            copy.wait_recv()
        for copy in sibling_copies(r, src):
            copy.start()

    early = units // 2
    loop(early, pass_on)
    loop(tp, share_page)

    def wait_page(j):
        src = (p + tp - j) % tp
        for copy in sibling_copies(1 - r, src):
            copy.wait_recv()

    loop(tp, wait_page)
    quads = tp // 4
    lane = lax.broadcasted_iota(jnp.int32, (rows, 4 * rank), 1) // rank

    def chosen(i):
        return source[...] == lane + i * 4

    def shrink_quad(i):
        pages = a_buf[i // quads, pl.ds((i % quads) * 4, 4)].reshape(4 * rank, a_buf.shape[3])
        value = lax.dot_general(
            hidden[...], pages, (((1,), (1,)), ((), ())), preferred_element_type=F32)
        part[...] += jnp.where(chosen(i), value, 0.0)

    part[...] = jnp.zeros_like(part)
    loop(2 * quads, shrink_quad)
    folded = part[:, :2 * rank] + part[:, 2 * rank:]
    folded = folded + jnp.concatenate([folded[:, rank:], folded[:, :rank]], axis=1)
    part[:, :2 * rank] = folded

    def rows_of(k):
        return pl.ds(pl.multiple_of(k * share, share), share)

    def part_copy(j):
        k = (p + j) % tp
        return remote(part.at[rows_of(k), pl.ds(0, 2 * rank)], part_in.at[p],
                      c_sems.at[0, k], c_sems.at[1, p], {"tp": k})

    def part_arrived(src):
        return remote(part.at[rows_of(src), pl.ds(0, 2 * rank)], part_in.at[src],
                      c_sems.at[0, src], c_sems.at[1, src], {"tp": src})

    def code_copy(k, at):
        return remote(code_own, code.at[rows_of(at)],
                      c_sems.at[2, k], c_sems.at[3, at], {"tp": k})

    loop(tp - 1, lambda j: part_copy(j + 1).start())
    loop(units - early, lambda i: pass_on(early + i))

    code_own[...] = part[rows_of(p), :2 * rank]

    def add_part(j):
        src = (p + j + 1) % tp
        part_arrived(src).wait_recv()
        code_own[...] += part_in[src]

    loop(tp - 1, add_part)
    code_own[...] = code_own[...].astype(BF16).astype(F32)
    code[rows_of(p), :] = code_own[...]
    loop(tp - 1, lambda j: code_copy((p + j + 1) % tp, p).start())
    loop(tp - 1, lambda j: code_copy((p + j + 1) % tp, (p + j + 1) % tp).wait_recv())

    out[...] = jnp.zeros_like(out)

    def expand_quad(i):
        both = code[...]
        codes = jnp.where(chosen(i), jnp.concatenate([both, both], axis=1), 0.0).astype(BF16)
        pages = e_buf[i // quads, pl.ds((i % quads) * 4, 4)].reshape(4 * rank, width)
        out[...] += jnp.dot(codes, pages, preferred_element_type=F32)

    loop(2 * quads, expand_quad)

    def finish(c):
        u = z * per + c
        columns = pl.ds(pl.multiple_of(c * tile, tile), tile)
        wait_y(u)
        out[:, columns] += base(u)

        @pl.when(z > 0)
        def _():
            z_arrived(u)
            out[:, columns] += z_recv[u].astype(F32)

        @pl.when(z < hi - 1)
        def _():
            z_arrived(units + c)
            out[:, columns] += z_recv[units + c].astype(F32)

    loop(per, finish)

    def sent(i):
        zz, c = unit(i)
        u = zz * per + c
        for j in range(1, lo):
            y_copy(u, j).wait_send()

        @pl.when(zz != z)
        def _():
            z_copy(u, zz, c).wait_send()

    loop(units, sent)

    def sent_pages(j):
        for copy in across_copies(j, mine) + sibling_copies(r, j):
            copy.wait_send()

        @pl.when(j > 0)
        def _():
            for copy in page_copies(j):
                copy.wait_send()
            part_copy(j).wait_send()
            code_copy((p + j) % tp, p).wait_send()

    loop(tp, sent_pages)


def per_device(
    hidden, down_weight, residual, pool_shrink, pool_expand, tenant_home, request_owner_tenant
):
    tp = lax.axis_size("tp")
    reps = lax.axis_size("rep")
    place = lax.axis_index("tp")
    requests, steps, units = hidden.shape
    width = residual.shape[2]
    rank = pool_shrink.shape[2]
    rows = requests * steps
    home_device = tenant_home // tp * tp + (tenant_home % tp + place) % tp
    tenants = tenant_home.shape[0]
    source = jnp.sum(
        jnp.where(request_owner_tenant == jnp.arange(tenants)[None, :], home_device[None, :], 0),
        axis=1, dtype=jnp.int32,
    )
    source = jnp.broadcast_to(source[:, None], (requests, steps)).reshape(rows, 1)
    lo = 1 << (int(math.log2(tp)) // 2)
    hi = tp // lo
    tile = min(512, width)
    sub = min(256, tile)
    per = width // tile
    n = hi * per
    dma = pltpu.SemaphoreType.DMA
    vmem = pl.BlockSpec(memory_space=pltpu.VMEM)
    hbm = pl.BlockSpec(memory_space=pl.ANY)
    added = pl.pallas_call(
        functools.partial(fused, tp, lo, hi, tile, sub),
        out_shape=jax.ShapeDtypeStruct((rows, width), F32),
        in_specs=[vmem, hbm, hbm, hbm, vmem],
        out_specs=vmem,
        scratch_shapes=[
            pltpu.VMEM((2, units, tile), BF16),
            pltpu.VMEM((n, lo - 1, rows, tile), BF16),
            pltpu.VMEM((n, lo - 1, rows, tile), BF16),
            pltpu.VMEM((n, rows, tile), F32),
            pltpu.VMEM((n, rows, tile), BF16),
            pltpu.VMEM((n + per, rows, tile), BF16),
            pltpu.VMEM((reps, tp, rank, units), BF16),
            pltpu.VMEM((reps, tp, rank, width), BF16),
            pltpu.VMEM((rows, 4 * rank), F32),
            pltpu.VMEM((tp, rows // tp, 2 * rank), F32),
            pltpu.VMEM((rows, 2 * rank), F32),
            pltpu.VMEM((rows // tp, 2 * rank), F32),
            dma((2,)),
            dma((n, lo - 1)),
            dma((n, lo - 1)),
            dma((n,)),
            dma((n + per,)),
            dma((6, tp)),
            dma((6, tp)),
            dma((4, tp)),
        ],
        compiler_params=pltpu.CompilerParams(
            collective_id=0, has_side_effects=True, vmem_limit_bytes=62 * 1024 * 1024
        ),
    )(hidden.reshape(rows, units), down_weight, pool_shrink, pool_expand, source)
    added = added.reshape(requests, steps, width)
    return (residual.astype(F32) + added).astype(BF16)


def solution(mesh):
    in_specs = (
        P(("groups", "rep"), None, "tp"),
        P("tp", None),
        P(("groups", "rep"), None, "tp"),
        P(("rep", "tp"), None, None, None),
        P(("rep", "tp"), None, None, None),
        P(),
        P(("groups", "rep"), None),
    )
    out_specs = P(("groups", "rep"), None, "tp")
    return jax.shard_map(
        per_device, mesh=mesh, in_specs=in_specs, out_specs=out_specs, check_vma=False
    )
```

time: 563 us -> 182 us (0.32)
  waiting for transfers between devices: 202 us -> 0 us
  Pallas kernels: 0 us -> 165 us
  blocking collectives: 151 us -> 0 us
  matrix products: 105 us -> 0 us
  local copies, waits for them, and re-layouts: 74.4 us -> 11.9 us
  between operations: 13.5 us -> 0.04 us
  other arithmetic: 10.2 us -> 3.49 us
    all_to_all x1 -> x0, waiting for transfers between devices: 202 us -> none  [per_device(): lax.all_to_all(shrink_flat, ('rep', 'tp'), split_axis=0, concat_axis=0, t...]
    pallas_call x0 -> x1, Pallas kernels: none -> 165 us  [per_device(): pl.pallas_call(functools.partial(fused, tp, lo, hi, tile, sub), out_shape...]
    dot_general x3 -> x0, matrix products: 105 us -> none  [the longest x1 51.1 us: per_device(): jnp.einsum('isf,ikf->isk', hidden, row_shrink, preferred_element_type=jnp...]
    all_to_all x1 -> x0, blocking collectives: 104 us -> none  [per_device(): lax.all_to_all(expand_flat, ('rep', 'tp'), split_axis=0, concat_axis=0, t...]
    gather x3 -> x0, local copies, waits for them, and re-layouts: 56.6 us -> none  [the longest x1 42.1 us: per_device(): row_shrink = received_shrink[source_device_of]]
    psum x1 -> x0, blocking collectives: 47.6 us -> none  [per_device(): codes = lax.psum(code_part, 'tp').astype(jnp.bfloat16)]
    gather x4 -> x0, other arithmetic: 10.2 us -> none  [the longest x3 10.2 us: per_device(): source_device_of = home_device[tenant_ids]]
    reshape x2 -> x3, local copies, waits for them, and re-layouts: 10.7 us -> 11.8 us  [the longest x1 8.4 us: per_device(): hidden.reshape(rows, units)]
  transfers between devices with their start and end apart: 2 -> 0, of which waited for: 1 -> 0; matrix products, arithmetic and copies ran while one was open for 22% -> 0% of each run, Pallas kernels for 0% -> 0%
where the time goes in v1:
time: 182 us; the launch traced here: 180 us
  Pallas kernels  165 us (91%)
  local copies, waits for them, and re-layouts  11.9 us (7%)
  other arithmetic  3.49 us (2%)
    pallas_call x1, Pallas kernels, per_device(): pl.pallas_call(functools.partial(fused, tp, lo, hi, tile, sub), out_shape...  165 us
    reshape x1, local copies, waits for them, and re-layouts, per_device(): hidden.reshape(rows, units)  8.4 us

profile of v1, /device:TPU:0, one launch (start us, length us, event | category | flops | bytes accessed | tf_op | source)
XLA Modules:
  0.0 180.3 jit_solution(9185327035868415206)
XLA Ops:
  0.0 0.7 fusion
  0.7 0.8 select_reduce_fusion
  1.4 0.1 broadcast_in_dim.22
  1.5 0.8 reshape.14.source
  2.4 8.4 %reshape.11.hidden = bf16[512,3584]{1,0:T(8,128)(2,1)} reshape(bf16[256,2,3584]{2,1,0:T(2,128)(2,1)} %param.7) | data formatting | bytes 7340032 | tf_op jit(solution)/shard_map/reshape | solution.py:391
  10.7 164.9 %shard_map.73 = f32[512,1024]{1,0:T(8,128)} custom-call(bf16[512,3584]{1,0:T(8,128)(2,1)} %reshape.11.hidden, bf16[3584,8192]{1,0:T(8,128)(2,1)} %weight.1, bf16[1,8,64,3584]{3,2,1,0:T(8,128)(2,1)} %shrink.1, bf16[1,8,64,1024]{3,2,1,0:T(8,128)(2,1)} %expand.1, s32[512,1]{1,0:T(8,128)} %reshape.14.source), custom_call_target="tpu_custom_call" | custom-call | tf_op jit(solution)/shard_map/pallas_call | solution.py:361
  175.6 0.0 copy-start
  175.6 2.6 %reshape.13 = f32[256,2,1024]{2,1,0:T(2,128)S(1)} reshape(f32[512,1024]{1,0:T(8,128)} %shard_map.73) | data formatting | bytes 4194304 | tf_op jit(solution)/shard_map/reshape | solution.py:392
  178.2 0.0 copy-done
  178.2 2.0 %add_convert_fusion = bf16[256,2,1024]{2,1,0:T(2,128)(2,1)} fusion(f32[256,2,1024]{2,1,0:T(2,128)S(1)} %reshape.13, bf16[256,2,1024]{2,1,0:T(2,128)(2,1)S(1)} %copy-done), kind=kLoop, calls=%fused_computation | loop fusion | flops 1572864 | bytes 4194304 | tf_op jit(solution)/shard_map/convert_element_type | solution.py:393
Async XLA Ops:
  175.6 2.6 %copy-start = (bf16[256,2,1024]{2,1,0:T(2,128)(2,1)S(1)}, bf16[256,2,1024]{2,1,0:T(2,128)(2,1)}, u32[]{:S(2)}) copy-start(bf16[256,2,1024]{2,1,0:T(2,128)(2,1)} %param.9) | copy-start | bytes 3145732

commit v2 on v1

--- a/solution.py
+++ b/solution.py
@@ -14,17 +14,18 @@
 
 
 def fused(
-    tp, lo, hi, tile, sub,
+    tp, lo, hi, tile, sub, zf,
     hidden, weight, shrink, expand, source, out,
-    w_buf, y_send, y_recv, keep, z_send, z_recv, a_buf, e_buf, part, part_in, code, code_own,
-    w_sem, y_ssem, y_rsem, z_ssem, z_rsem, a_sems, e_sems, c_sems,
+    w_buf, y_send, y_recv, keep, z_send, z_recv, f_own, f_send, f_recv, fy_send, fy_recv, a_buf, e_buf, part, part_in, code, code_own,
+    w_sem, y_ssem, y_rsem, z_ssem, z_rsem, f_ssem, f_rsem, fy_sems, a_sems, e_sems, c_sems,
 ):
     g, r, p = lax.axis_index("groups"), lax.axis_index("rep"), lax.axis_index("tp")
     z, y = p // lo, p % lo
     rows = hidden.shape[0]
     width = out.shape[1]
-    per = width // tile
+    per = width // tile - zf
     units = hi * per
+    firsts = tp * zf
     rank = shrink.shape[2]
     half = rank // 2
     share = rows // tp
@@ -48,26 +49,36 @@
     pl.semaphore_signal(barrier, inc=1, device_id=across, device_id_type=MESH)
     pl.semaphore_signal(barrier, inc=1, device_id=sibling, device_id_type=MESH)
 
+    def far(q):
+        return jnp.where(q % 2 == 0, hi - 1 - q // 2, q // 2)
+
     def unit(i):
-        q, c = i // per, i % per
-        zz = jnp.where(q % 2 == 0, hi - 1 - q // 2, q // 2)
-        return zz, c
+        return far(i // per), i % per
+
+    def first_unit(m):
+        rest = m % (lo * zf)
+        return far(m // (lo * zf)), rest // zf, rest % zf
 
     sends = units * (lo - 1)
-    total = units * lo
-
-    def tile_of(n):
+    total = units * lo + firsts
+
+    def column_of(n):
         sending = n < sends
-        i = jnp.where(sending, n // max(lo - 1, 1), n - sends)
-        j = jnp.where(sending, 1 + n % max(lo - 1, 1), 0)
+        i = jnp.where(sending, n // (lo - 1), jnp.maximum(n - sends - firsts, 0))
         zz, c = unit(i)
-        return zz, c, j
+        yy = jnp.where(sending, (y + 1 + n % (lo - 1)) % lo, y)
+        if zf:
+            m = jnp.clip(n - sends, 0, firsts - 1)
+            fz, fy, fc = first_unit(m)
+            inside = jnp.logical_and(n >= sends, n < sends + firsts)
+            zz = jnp.where(inside, fz, zz)
+            yy = jnp.where(inside, fy, yy)
+            c = jnp.where(inside, per + fc, c)
+        return (zz * lo + yy) * width + c * tile
 
     def w_copy(n):
-        zz, c, j = tile_of(n)
-        column = (zz * lo + (y + j) % lo) * width + c * tile
         return pltpu.make_async_copy(
-            weight.at[:, pl.ds(pl.multiple_of(column, tile), tile)],
+            weight.at[:, pl.ds(pl.multiple_of(column_of(n), tile), tile)],
             w_buf.at[n % 2], w_sem.at[n % 2],
         )
 
@@ -131,7 +142,8 @@
                       y_ssem.at[u, j - 1], y_rsem.at[u, j - 1], device)
 
     def send_tile(n):
-        zz, c, j = tile_of(n)
+        zz, c = unit(n // (lo - 1))
+        j = 1 + n % (lo - 1)
         u = zz * per + c
 
         def store(columns, value):
@@ -159,6 +171,93 @@
         for copy in across_copies(src, mine):
             copy.start()
 
+    def forward_some(t):
+        steps = firsts + units
+        lax.fori_loop(
+            t * tp // steps, (t + 1) * tp // steps, lambda j, c: (forward(j), c)[1], 0)
+
+    def step(u, zz, buf_s, buf_r, ssem, rsem, slot, value):
+        start = jnp.where(zz > z, z == 0, z == hi - 1)
+
+        @pl.when(start)
+        def _():
+            buf_s[u] = value().astype(BF16)
+
+        @pl.when(jnp.logical_not(start))
+        def _():
+            arrived(buf_s, buf_r, ssem, rsem, u)
+            buf_s[u] = (value() + buf_r[u].astype(F32)).astype(BF16)
+
+        step_copy(u, zz, buf_s, buf_r, ssem, rsem, slot).start()
+
+    def step_copy(u, zz, buf_s, buf_r, ssem, rsem, slot):
+        nz = jnp.where(zz > z, z + 1, z - 1)
+        target = jnp.where(jnp.logical_and(nz == zz, zz < z), slot, u)
+        return remote(buf_s.at[u], buf_r.at[target], ssem.at[u], rsem.at[target],
+                      {"tp": nz * lo + y})
+
+    def arrived(buf_s, buf_r, ssem, rsem, slot):
+        remote(buf_s.at[0], buf_r.at[slot], ssem.at[0], rsem.at[slot], across).wait_recv()
+
+    def ends(buf_s, buf_r, ssem, rsem, u, slot, add):
+        @pl.when(z > 0)
+        def _():
+            arrived(buf_s, buf_r, ssem, rsem, u)
+            add(buf_r[u].astype(F32))
+
+        @pl.when(z < hi - 1)
+        def _():
+            arrived(buf_s, buf_r, ssem, rsem, slot)
+            add(buf_r[slot].astype(F32))
+
+    firsts_of = (f_send, f_recv, f_ssem, f_rsem)
+
+    def first_tile(m):
+        zz, yy, c = first_unit(m)
+        v = (zz * lo + yy) * zf + c
+
+        def store(columns, value):
+            f_own[v, :, columns] = value
+
+        product(sends + m, store)
+        forward_some(m)
+
+    def first_step(m):
+        zz, yy, c = first_unit(m)
+        v = (zz * lo + yy) * zf + c
+
+        @pl.when(zz != z)
+        def _():
+            step(v, zz, *firsts_of, firsts + yy * zf + c, lambda: f_own[v])
+
+    def first_ends(yy, c):
+        v = (z * lo + yy) * zf + c
+
+        def add(value):
+            f_own[v] += value
+
+        ends(*firsts_of, v, firsts + yy * zf + c, add)
+        return v
+
+    def fy_copy(c, j):
+        return remote(fy_send.at[c, j - 1], fy_recv.at[c, j - 1],
+                      fy_sems.at[0, c, j - 1], fy_sems.at[1, c, j - 1],
+                      {"tp": z * lo + (y + j) % lo})
+
+    def first_across(i):
+        c, j = i // (lo - 1), 1 + i % (lo - 1)
+        v = first_ends((y + j) % lo, c)
+        fy_send[c, j - 1] = f_own[v].astype(BF16)
+        fy_copy(c, j).start()
+
+    def first_finish(c):
+        columns = pl.ds(pl.multiple_of((per + c) * tile, tile), tile)
+        v = first_ends(y, c)
+        out[:, columns] += f_own[v]
+        for j in range(1, lo):
+            fy_copy(c, j).wait_recv()
+            out[:, columns] += fy_recv[c, j - 1].astype(F32)
+
     def keep_tile(i):
         zz, c = unit(i)
         u = zz * per + c
@@ -166,10 +265,14 @@
         def store(columns, value):
             keep[u, :, columns] = value
 
-        product(sends + i, store)
-        loop(tp // units, lambda t: forward(i * (tp // units) + t))
-
+        product(sends + firsts + i, store)
+        forward_some(firsts + i)
+
+    if zf:
+        loop(firsts, first_tile)
     loop(units, keep_tile)
+    if zf:
+        loop(firsts, first_step)
 
     def base(u):
         value = keep[u]
@@ -181,35 +284,16 @@
         for j in range(1, lo):
             y_copy(u, j).wait_recv()
 
-    def z_copy(u, zz, c):
-        nz = jnp.where(zz > z, z + 1, z - 1)
-        slot = jnp.where((nz == zz) & (zz < z), units + c, u)
-        return remote(z_send.at[u], z_recv.at[slot], z_ssem.at[u], z_rsem.at[slot],
-                      {"tp": nz * lo + y})
-
-    def z_arrived(slot):
-        remote(z_send.at[0], z_recv.at[slot], z_ssem.at[0], z_rsem.at[slot],
-               across).wait_recv()
+    units_of = (z_send, z_recv, z_ssem, z_rsem)
 
     def pass_on(i):
         zz, c = unit(i)
         u = zz * per + c
-        first = jnp.where(zz > z, z == 0, z == hi - 1)
 
         @pl.when(zz != z)
         def _():
             wait_y(u)
-
-            @pl.when(first)
-            def _():
-                z_send[u] = base(u).astype(BF16)
-
-            @pl.when(jnp.logical_not(first))
-            def _():
-                z_arrived(u)
-                z_send[u] = (base(u) + z_recv[u].astype(F32)).astype(BF16)
-
-            z_copy(u, zz, c).start()
+            step(u, zz, *units_of, units + c, lambda: base(u))
 
     def share_page(j):
         src = (p + tp - j) % tp
@@ -220,6 +304,8 @@
 
     early = units // 2
     loop(early, pass_on)
+    if zf:
+        loop(zf * (lo - 1), first_across)
     loop(tp, share_page)
 
     def wait_page(j):
@@ -241,7 +327,15 @@
         part[...] += jnp.where(chosen(i), value, 0.0)
 
     part[...] = jnp.zeros_like(part)
-    loop(2 * quads, shrink_quad)
+    middle = (units - early) * 2 // 3
+
+    def quads_and_unit(t):
+        lax.fori_loop(
+            t * 2 * quads // middle, (t + 1) * 2 * quads // middle,
+            lambda i, c: (shrink_quad(i), c)[1], 0)
+        pass_on(early + t)
+
+    loop(middle, quads_and_unit)
     folded = part[:, :2 * rank] + part[:, 2 * rank:]
     folded = folded + jnp.concatenate([folded[:, rank:], folded[:, :rank]], axis=1)
     part[:, :2 * rank] = folded
@@ -263,7 +357,7 @@
                       c_sems.at[2, k], c_sems.at[3, at], {"tp": k})
 
     loop(tp - 1, lambda j: part_copy(j + 1).start())
-    loop(units - early, lambda i: pass_on(early + i))
+    loop(units - early - middle, lambda i: pass_on(early + middle + i))
 
     code_own[...] = part[rows_of(p), :2 * rank]
 
@@ -294,16 +388,13 @@
         wait_y(u)
         out[:, columns] += base(u)
 
-        @pl.when(z > 0)
-        def _():
-            z_arrived(u)
-            out[:, columns] += z_recv[u].astype(F32)
-
-        @pl.when(z < hi - 1)
-        def _():
-            z_arrived(units + c)
-            out[:, columns] += z_recv[units + c].astype(F32)
-
+        def add(value):
+            out[:, columns] += value
+
+        ends(*units_of, u, units + c, add)
+
+    if zf:
+        loop(zf, first_finish)
     loop(per, finish)
 
     def sent(i):
@@ -314,9 +405,21 @@
 
         @pl.when(zz != z)
         def _():
-            z_copy(u, zz, c).wait_send()
+            step_copy(u, zz, *units_of, units + c).wait_send()
 
     loop(units, sent)
+
+    def first_sent(m):
+        zz, yy, c = first_unit(m)
+        v = (zz * lo + yy) * zf + c
+
+        @pl.when(zz != z)
+        def _():
+            step_copy(v, zz, *firsts_of, firsts + yy * zf + c).wait_send()
+
+    if zf:
+        loop(firsts, first_sent)
+        loop(zf * (lo - 1), lambda i: fy_copy(i // (lo - 1), 1 + i % (lo - 1)).wait_send())
 
     def sent_pages(j):
         for copy in across_copies(j, mine) + sibling_copies(r, j):
@@ -351,15 +454,18 @@
     source = jnp.broadcast_to(source[:, None], (requests, steps)).reshape(rows, 1)
     lo = 1 << (int(math.log2(tp)) // 2)
     hi = tp // lo
-    tile = min(512, width)
+    tile = max(128, width // 4)
     sub = min(256, tile)
-    per = width // tile
+    zf = width // tile // 4
+    per = width // tile - zf
     n = hi * per
+    few = max(zf, 1)
+    m = tp * few
     dma = pltpu.SemaphoreType.DMA
     vmem = pl.BlockSpec(memory_space=pltpu.VMEM)
     hbm = pl.BlockSpec(memory_space=pl.ANY)
     added = pl.pallas_call(
-        functools.partial(fused, tp, lo, hi, tile, sub),
+        functools.partial(fused, tp, lo, hi, tile, sub, zf),
         out_shape=jax.ShapeDtypeStruct((rows, width), F32),
         in_specs=[vmem, hbm, hbm, hbm, vmem],
         out_specs=vmem,
@@ -370,6 +476,11 @@
             pltpu.VMEM((n, rows, tile), F32),
             pltpu.VMEM((n, rows, tile), BF16),
             pltpu.VMEM((n + per, rows, tile), BF16),
+            pltpu.VMEM((m, rows, tile), F32),
+            pltpu.VMEM((m, rows, tile), BF16),
+            pltpu.VMEM((m + lo * few, rows, tile), BF16),
+            pltpu.VMEM((few, lo - 1, rows, tile), BF16),
+            pltpu.VMEM((few, lo - 1, rows, tile), BF16),
             pltpu.VMEM((reps, tp, rank, units), BF16),
             pltpu.VMEM((reps, tp, rank, width), BF16),
             pltpu.VMEM((rows, 4 * rank), F32),
@@ -381,6 +492,9 @@
             dma((n, lo - 1)),
             dma((n,)),
             dma((n + per,)),
+            dma((m,)),
+            dma((m + lo * few,)),
+            dma((2, few, lo - 1)),
             dma((6, tp)),
             dma((6, tp)),
             dma((4, tp)),

time: 182 us -> 194 us (1.066)
  Pallas kernels: 165 us -> 178 us
    pallas_call x1, Pallas kernels: 165 us -> 178 us  [per_device(): pl.pallas_call(functools.partial(fused, tp, lo, hi, tile, sub, zf), out_s...]
where the time goes in v2:
time: 194 us; the launch traced here: 193 us
  Pallas kernels  178 us (92%)
  local copies, waits for them, and re-layouts  11.9 us (6%)
  other arithmetic  3.49 us (2%)
    pallas_call x1, Pallas kernels, per_device(): pl.pallas_call(functools.partial(fused, tp, lo, hi, tile, sub, zf), out_s...  178 us
    reshape x1, local copies, waits for them, and re-layouts, per_device(): hidden.reshape(rows, units)  8.4 us

profile of v2, /device:TPU:0, one launch (start us, length us, event | category | flops | bytes accessed | tf_op | source)
XLA Modules:
  0.0 193.3 jit_solution(8160389408085380770)
XLA Ops:
  0.0 0.7 fusion
  0.7 0.8 select_reduce_fusion
  1.4 0.1 broadcast_in_dim.22
  1.5 0.8 reshape.14.source
  2.4 8.4 %reshape.11.hidden = bf16[512,3584]{1,0:T(8,128)(2,1)} reshape(bf16[256,2,3584]{2,1,0:T(2,128)(2,1)} %param.7) | data formatting | bytes 7340032 | tf_op jit(solution)/shard_map/reshape | solution.py:505
  10.7 177.9 %shard_map.73 = f32[512,1024]{1,0:T(8,128)} custom-call(bf16[512,3584]{1,0:T(8,128)(2,1)} %reshape.11.hidden, bf16[3584,8192]{1,0:T(8,128)(2,1)} %weight.1, bf16[1,8,64,3584]{3,2,1,0:T(8,128)(2,1)} %shrink.1, bf16[1,8,64,1024]{3,2,1,0:T(8,128)(2,1)} %expand.1, s32[512,1]{1,0:T(8,128)} %reshape.14.source), custom_call_target="tpu_custom_call" | custom-call | tf_op jit(solution)/shard_map/pallas_call | solution.py:467
  188.7 0.0 copy-start
  188.7 2.6 %reshape.13 = f32[256,2,1024]{2,1,0:T(2,128)S(1)} reshape(f32[512,1024]{1,0:T(8,128)} %shard_map.73) | data formatting | bytes 4194304 | tf_op jit(solution)/shard_map/reshape | solution.py:506
  191.3 0.0 copy-done
  191.3 2.0 %add_convert_fusion = bf16[256,2,1024]{2,1,0:T(2,128)(2,1)} fusion(f32[256,2,1024]{2,1,0:T(2,128)S(1)} %reshape.13, bf16[256,2,1024]{2,1,0:T(2,128)(2,1)S(1)} %copy-done), kind=kLoop, calls=%fused_computation | loop fusion | flops 1572864 | bytes 4194304 | tf_op jit(solution)/shard_map/convert_element_type | solution.py:507
Async XLA Ops:
  188.7 2.6 %copy-start = (bf16[256,2,1024]{2,1,0:T(2,128)(2,1)S(1)}, bf16[256,2,1024]{2,1,0:T(2,128)(2,1)}, u32[]{:S(2)}) copy-start(bf16[256,2,1024]{2,1,0:T(2,128)(2,1)} %param.9) | copy-start | bytes 3145732

commit v3 on v1

--- a/solution.py
+++ b/solution.py
@@ -221,6 +221,8 @@
     early = units // 2
     loop(early, pass_on)
     loop(tp, share_page)
+    later = units // 4
+    loop(later, lambda i: pass_on(early + i))
 
     def wait_page(j):
         src = (p + tp - j) % tp
@@ -263,7 +265,7 @@
                       c_sems.at[2, k], c_sems.at[3, at], {"tp": k})
 
     loop(tp - 1, lambda j: part_copy(j + 1).start())
-    loop(units - early, lambda i: pass_on(early + i))
+    loop(units - early - later, lambda i: pass_on(early + later + i))
 
     code_own[...] = part[rows_of(p), :2 * rank]
 

time: 182 us -> 180 us (0.989)
  no operation moved by 1% of the time
where the time goes in v3:
time: 180 us
  Pallas kernels  164 us (91%)
  local copies, waits for them, and re-layouts  11.9 us (7%)
  other arithmetic  3.49 us (2%)
    pallas_call x1, Pallas kernels, per_device(): pl.pallas_call(functools.partial(fused, tp, lo, hi, tile, sub), out_shape...  164 us
    reshape x1, local copies, waits for them, and re-layouts, per_device(): hidden.reshape(rows, units)  8.4 us

profile of v3, /device:TPU:0, one launch (start us, length us, event | category | flops | bytes accessed | tf_op | source)
XLA Modules:
  0.0 179.9 jit_solution(17303765645931720409)
XLA Ops:
  0.0 0.7 fusion
  0.7 0.8 select_reduce_fusion
  1.4 0.1 broadcast_in_dim.22
  1.5 0.8 reshape.14.source
  2.4 8.4 %reshape.11.hidden = bf16[512,3584]{1,0:T(8,128)(2,1)} reshape(bf16[256,2,3584]{2,1,0:T(2,128)(2,1)} %param.7) | data formatting | bytes 7340032 | tf_op jit(solution)/shard_map/reshape | solution.py:393
  10.7 164.5 %shard_map.73 = f32[512,1024]{1,0:T(8,128)} custom-call(bf16[512,3584]{1,0:T(8,128)(2,1)} %reshape.11.hidden, bf16[3584,8192]{1,0:T(8,128)(2,1)} %weight.1, bf16[1,8,64,3584]{3,2,1,0:T(8,128)(2,1)} %shrink.1, bf16[1,8,64,1024]{3,2,1,0:T(8,128)(2,1)} %expand.1, s32[512,1]{1,0:T(8,128)} %reshape.14.source), custom_call_target="tpu_custom_call" | custom-call | tf_op jit(solution)/shard_map/pallas_call | solution.py:363
  175.2 0.0 copy-start
  175.2 2.6 %reshape.13 = f32[256,2,1024]{2,1,0:T(2,128)S(1)} reshape(f32[512,1024]{1,0:T(8,128)} %shard_map.73) | data formatting | bytes 4194304 | tf_op jit(solution)/shard_map/reshape | solution.py:394
  177.8 0.0 copy-done
  177.8 2.0 %add_convert_fusion = bf16[256,2,1024]{2,1,0:T(2,128)(2,1)} fusion(f32[256,2,1024]{2,1,0:T(2,128)S(1)} %reshape.13, bf16[256,2,1024]{2,1,0:T(2,128)(2,1)S(1)} %copy-done), kind=kLoop, calls=%fused_computation | loop fusion | flops 1572864 | bytes 4194304 | tf_op jit(solution)/shard_map/convert_element_type | solution.py:395
Async XLA Ops:
  175.2 2.6 %copy-start = (bf16[256,2,1024]{2,1,0:T(2,128)(2,1)S(1)}, bf16[256,2,1024]{2,1,0:T(2,128)(2,1)}, u32[]{:S(2)}) copy-start(bf16[256,2,1024]{2,1,0:T(2,128)(2,1)} %param.9) | copy-start | bytes 3145732
